TPU v7x, 32 devices: a whole 2x2x4 slice. The times are simulated.
32 devices in a mesh: occ: 2 (over x), vir: 16 (over z, y, core).
Axes of the slice: x: 2, y: 2, z: 4, core: 2. Of those that a mesh axis runs over, the one named last changes fastest.
Arguments:
- amplitudes: bfloat16 [256, 240, 2112], P(('occ', 'vir')), may hold values from -6 to 6
- integrals: bfloat16 [240, 2112, 256], P('occ', 'vir'), may hold values from -0.01171875 to 0.01171875
- screen: int32 [5, 22], replicated, may hold values 0 or 1
- row_gap: float32 [256], P('occ'), may hold values from 0.2 to 2
- col_gap: float32 [256], P('vir'), may hold values from 0.2 to 2
Outputs:
- update: float32 [256, 256], P('occ', 'vir')
Inputs may be any that keep to these rules, and one draw needn't show every extreme that they name: `screen`: 1 keeps the amplitudes of an occupied tile and a virtual tile, 0 screens them out.
All inputs are finite; a program needn't handle non-finite values.
Results may differ from a plain program's by a relative error of at most 0.0003.
Values may be sent and summed in bfloat16 or wider, within the bound.
A program may use at most 128 MiB of HBM per device.

v0:
```python
import jax
import jax.numpy as jnp
from jax import lax
from jax.sharding import PartitionSpec as P


def shards(amplitudes, integrals, screen, row_gap, col_gap):
    rows_here, occ_all, vir_all = amplitudes.shape
    tiles_occ, tiles_vir = screen.shape
    keep_mask = jnp.broadcast_to(
        screen.astype(jnp.bfloat16)[:, None, :, None],
        (tiles_occ, occ_all // tiles_occ, tiles_vir, vir_all // tiles_vir),
    ).reshape(occ_all, vir_all)
    screened = amplitudes * keep_mask[None]
    occ_part, vir_part, col_total = integrals.shape
    relaid = lax.all_to_all(
        lax.all_to_all(screened[None, None], "occ", split_axis=3, concat_axis=0, tiled=True),
        "vir",
        split_axis=4,
        concat_axis=1,
        tiled=True,
    )
    flat_rows = relaid.reshape(-1, occ_part * vir_part)
    int_slab = integrals.reshape(occ_part * vir_part, col_total)
    per_vir = lax.psum_scatter(
        lax.dot_general(
            int_slab, flat_rows, (((0,), (1,)), ((), ())), preferred_element_type=jnp.float32
        ),
        "vir",
        scatter_dimension=0,
        tiled=True,
    )
    cycle_cols = lax.psum_scatter(per_vir, "occ", scatter_dimension=1, tiled=True)
    cycle_sum = cycle_cols.T
    update = cycle_sum / (row_gap[:, None] + col_gap[None, :])
    return update


def solution(mesh):
    placed = (P(("occ", "vir"), None, None), P("occ", "vir", None), P(), P("occ"), P("vir"))
    return jax.shard_map(
        shards, mesh=mesh, in_specs=placed, out_specs=P("occ", "vir"), check_vma=False
    )
```

profile of v0, /device:TPU:0, one launch (start us, length us, event | category | flops | bytes accessed | tf_op | source)
XLA Modules:
  0.0 464.6 jit_solution(2814639098561962855)
XLA Ops:
  6.5 0.7 convert_element_type.3
  7.2 0.3 broadcast_in_dim.4
  7.5 1.0 mul.10
  8.5 7.6 %fusion = bf16[1,1,8,240,2112]{4,2,1,0,3:T(8,128)(2,1)S(1)} fusion(bf16[8,240,2112]{2,1,0:T(8,128)(2,1)} %param.5, bf16[240,2112]{1,0:T(8,128)(2,1)S(1)} %mul.10), kind=kLoop, calls=%fused_computation.1 | loop fusion | flops 4055040 | bytes 17233920 | tf_op jit(solution)/shard_map/broadcast_in_dim | solution.py:17
  16.1 97.7 %all_to_all.33 = bf16[1,1,8,240,2112]{4,2,1,0,3:T(8,128)(2,1)} all-to-all(bf16[1,1,8,240,2112]{4,2,1,0,3:T(8,128)(2,1)S(1)} %fusion), channel_id=1, replica_groups=mesh['occ'=2,'vir'=16] {'occ'}, dimensions={3} | all-to-all | bytes 16220160 | tf_op jit(solution)/shard_map/all_to_all | solution.py:17
  113.9 7.6 %copy.22 = bf16[1,1,8,240,2112]{4,3,2,1,0:T(8,128)(2,1)} copy(bf16[1,1,8,240,2112]{4,2,1,0,3:T(8,128)(2,1)} %all_to_all.33) | data formatting | bytes 16220160 | tf_op jit(solution)/shard_map/all_to_all | solution.py:17
  121.5 22.5 %copy.23 = bf16[2,1,8,120,2112]{3,0,2,1,4:T(2,128)(2,1)} copy(bf16[2,1,8,120,2112]{4,3,0,2,1:T(8,128)(2,1)} %bitcast.22) | data formatting | bytes 16220160 | tf_op jit(solution)/shard_map/all_to_all | solution.py:17
  143.9 6.2 %all-to-all-start.1 = ((bf16[2,1,8,120,2112]{3,0,2,1,4:T(2,128)(2,1)}), bf16[2,1,8,120,2112]{3,0,2,1,4:T(2,128)(2,1)}, u32[]{:S(2)}, u32[]{:S(2)}) async-start(bf16[2,1,8,120,2112]{3,0,2,1,4:T(2,128)(2,1)} %copy.23), calls=%async_computation.1 | async-start | bytes 17301504 | tf_op jit(solution)/shard_map/all_to_all | solution.py:16
  150.2 0.0 reduce-scatter.7.cloned.1.call-start
  150.2 8.2 %copy.26 = bf16[120,132,256]{2,1,0:T(8,128)(2,1)} copy(bf16[120,132,256]{2,0,1:T(8,128)(2,1)} %param.6) | data formatting | bytes 16220160 | tf_op args[1]
  158.5 11.9 %reshape.12 = bf16[15840,256]{1,0:T(8,128)(2,1)} reshape(bf16[120,132,256]{2,1,0:T(8,128)(2,1)} %copy.26) | data formatting | bytes 16220160 | tf_op jit(solution)/shard_map/reshape | solution.py:24
  170.4 135.1 %all-to-all-done.1 = bf16[2,1,8,120,2112]{3,0,2,1,4:T(2,128)(2,1)} async-done(((bf16[2,1,8,120,2112]{3,0,2,1,4:T(2,128)(2,1)}), bf16[2,1,8,120,2112]{3,0,2,1,4:T(2,128)(2,1)}, u32[]{:S(2)}, u32[]{:S(2)}) %all-to-all-start.1) | async-done | bytes 8110112 | tf_op jit(solution)/shard_map/all_to_all | solution.py:16
  305.5 7.9 %copy.24 = bf16[2,1,8,120,2112]{3,2,4,0,1:T(8,128)(2,1)} copy(bf16[2,1,8,120,2112]{3,0,2,1,4:T(2,128)(2,1)} %all-to-all-done.1) | data formatting | bytes 16220160 | tf_op jit(solution)/shard_map/all_to_all | solution.py:16
  313.4 15.9 %copy.25 = bf16[2,16,1,8,120,132]{5,4,3,1,0,2:T(8,128)(2,1)} copy(bf16[2,16,1,8,120,132]{4,3,5,1,0,2:T(8,128)(2,1)} %bitcast.21) | data formatting | bytes 16220160 | tf_op jit(solution)/shard_map/all_to_all | solution.py:16
  329.2 20.0 %reshape.11 = bf16[256,15840]{1,0:T(8,128)(2,1)} reshape(bf16[2,16,1,8,120,132]{5,4,3,1,0,2:T(8,128)(2,1)} %copy.25) | data formatting | bytes 16220160 | tf_op jit(solution)/shard_map/reshape | solution.py:23
  349.2 0.0 copy-start
  349.2 0.0 copy-start.1
  349.2 7.9 %convolution_bitcast_fusion = f32[256,256]{0,1:T(8,128)S(1)} fusion(bf16[256,15840]{1,0:T(8,128)(2,1)} %reshape.11, bf16[15840,256]{1,0:T(8,128)(2,1)} %reshape.12), kind=kOutput, calls=%fused_computation.2 | convolution fusion | flops 2076180480 | bytes 16482304 | tf_op jit(solution)/shard_map/dot_general | solution.py:26
  357.1 0.8 copy.28
  357.9 0.0 reduce-scatter.7.cloned.1.call-update
  357.9 0.0 reduce-scatter.5.cloned.1.call-start
  358.0 87.3 %reduce-scatter.7.cloned.1.call-done = f32[16,256]{1,0:T(8,128)} async-done(((f32[256,256]{1,0:T(8,128)}), f32[16,256]{1,0:T(8,128)}) %reduce-scatter.7.cloned.1.call-update) | async-done | bytes 16400 | tf_op jit(solution)/shard_map/reduce_scatter | solution.py:25
  445.3 0.0 reduce-scatter.5.cloned.1.call-update
  445.3 11.0 %reduce-scatter.5.cloned.1.call-done = f32[16,128]{1,0:T(8,128)} async-done(((f32[16,256]{1,0:T(8,128)}), f32[16,128]{1,0:T(8,128)}) %reduce-scatter.5.cloned.1.call-update) | async-done | bytes 8208 | tf_op jit(solution)/shard_map/reduce_scatter | solution.py:33
  456.3 0.0 copy-done
  456.3 0.0 copy-done.1
  456.3 1.4 bitcast_divide_fusion
Async XLA Ops:
  143.9 161.5 %all-to-all-start.1 = ((bf16[2,1,8,120,2112]{3,0,2,1,4:T(2,128)(2,1)}), bf16[2,1,8,120,2112]{3,0,2,1,4:T(2,128)(2,1)}, u32[]{:S(2)}, u32[]{:S(2)}) async-start(bf16[2,1,8,120,2112]{3,0,2,1,4:T(2,128)(2,1)} %copy.23), calls=%async_computation.1 | async-start | bytes 17301504 | tf_op jit(solution)/shard_map/all_to_all | solution.py:16
  150.2 295.1 %reduce-scatter.7.cloned.1.call-start = ((), (), s32[]{:S(2)}) async-start(), calls=%async_computation.5 | async-start | bytes 278528 | tf_op jit(solution)/shard_map/reduce_scatter | solution.py:25
  349.2 107.2 %copy-start = (f32[16]{0:T(128)S(1)}, f32[16]{0:T(128)}, u32[]{:S(2)}) copy-start(f32[16]{0:T(128)} %param.9) | copy-start | bytes 196
  349.2 107.2 %copy-start.1 = (f32[128]{0:T(128)S(1)}, f32[128]{0:T(128)}, u32[]{:S(2)}) copy-start(f32[128]{0:T(128)} %param.8) | copy-start | bytes 1540
  357.9 98.4 %reduce-scatter.5.cloned.1.call-start = ((), (), s32[]{:S(2)}) async-start(), calls=%async_computation.4 | async-start | bytes 24576 | tf_op jit(solution)/shard_map/reduce_scatter | solution.py:33
Sparse Core Ops, SparseCore 0:
  358.1 87.2 reduce-scatter.6
  447.5 8.7 reduce-scatter.4
where the time goes:
time: 467 us; the launch traced here: 465 us
  waiting for transfers between devices  233 us (50%)
  blocking collectives  97.7 us (21%)
  local copies, waits for them, and re-layouts  96.1 us (21%)
  between operations  13.5 us (3%)
  other arithmetic  9.62 us (2%)
  matrix products  7.89 us (2%)
  starting transfers between devices  6.32 us (1%)
    all_to_all x1, waiting for transfers between devices, shards(): lax.all_to_all(lax.all_to_all(screened[None, None], 'occ', split_axis=3,...  135 us
    all_to_all x1, blocking collectives, shards(): lax.all_to_all(screened[None, None], 'occ', split_axis=3, concat_axis=0,...  97.7 us
    reduce_scatter x1, waiting for transfers between devices, shards(): lax.psum_scatter(lax.dot_general(int_slab, flat_rows, (((0,), (1,)), ((),...  87.3 us
    all_to_all x2, local copies, waits for them, and re-layouts, shards(): lax.all_to_all(screened[None, None], 'occ', split_axis=3, concat_axis=0,...  30.1 us
    all_to_all x2, local copies, waits for them, and re-layouts, shards(): lax.all_to_all(lax.all_to_all(screened[None, None], 'occ', split_axis=3,...  23.7 us
    reshape x1, local copies, waits for them, and re-layouts, shards(): flat_rows = relaid.reshape(-1, occ_part * vir_part)  20 us
    reshape x1, local copies, waits for them, and re-layouts, shards(): int_slab = integrals.reshape(occ_part * vir_part, col_total)  11.9 us
    reduce_scatter x1, waiting for transfers between devices, shards(): lax.psum_scatter(per_vir, 'occ', scatter_dimension=1, tiled=True)  11 us
  transfers between devices with their start and end apart: 3, of which 3 were waited for; matrix products, arithmetic and copies ran while one was open for 4% of the time, Pallas kernels for 0%

commit v1 on v0

--- a/solution.py
+++ b/solution.py
@@ -2,6 +2,15 @@
 import jax.numpy as jnp
 from jax import lax
 from jax.sharding import PartitionSpec as P
+
+
+def update_core(t0, a_name):
+    return jnp.concatenate(
+        lax.all_to_all(
+            jnp.stack(jnp.split(t0, lax.axis_size(a_name), axis=3), axis=0), a_name, 0, 0
+        ),
+        axis=0,
+    )
 
 
 def shards(amplitudes, integrals, screen, row_gap, col_gap):
@@ -14,11 +23,7 @@
     screened = amplitudes * keep_mask[None]
     occ_part, vir_part, col_total = integrals.shape
     relaid = lax.all_to_all(
-        lax.all_to_all(screened[None, None], "occ", split_axis=3, concat_axis=0, tiled=True),
-        "vir",
-        split_axis=4,
-        concat_axis=1,
-        tiled=True,
+        update_core(screened[None, None], "occ"), "vir", split_axis=4, concat_axis=1, tiled=True
     )
     flat_rows = relaid.reshape(-1, occ_part * vir_part)
     int_slab = integrals.reshape(occ_part * vir_part, col_total)

time: 467 us -> 466 us (level)
  local copies, waits for them, and re-layouts: 96.1 us -> 82.8 us
  blocking collectives: 97.7 us -> 104 us
  other arithmetic: 9.62 us -> 15.8 us
    all_to_all x4 -> x2, local copies, waits for them, and re-layouts: 53.8 us -> 23.1 us  [shards(): lax.all_to_all(update_core(screened[None, None], 'occ'), 'vir', split_axi...]
    reshape x0 -> x1, local copies, waits for them, and re-layouts: none -> 12.5 us  [update_core(): jnp.concatenate(lax.all_to_all(jnp.stack(jnp.split(t0, lax.axis_size(a_na...]
    all_to_all x1, blocking collectives: 97.7 us -> 104 us  [update_core(): lax.all_to_all(jnp.stack(jnp.split(t0, lax.axis_size(a_name), axis=3), ax...]
    another operation x0 -> x1, other arithmetic: none -> 6.28 us  [update_core(): jnp.stack(jnp.split(t0, lax.axis_size(a_name), axis=3), axis=0)]
    another operation x0 -> x1, local copies, waits for them, and re-layouts: none -> 5.05 us  [update_core(): jnp.stack(jnp.split(t0, lax.axis_size(a_name), axis=3), axis=0)]
where the time goes in v1:
time: 466 us; the launch traced here: 464 us
  waiting for transfers between devices  233 us (50%)
  blocking collectives  104 us (22%)
  local copies, waits for them, and re-layouts  82.8 us (18%)
  other arithmetic  15.8 us (3%)
  between operations  13.4 us (3%)
  matrix products  7.89 us (2%)
  starting transfers between devices  6.33 us (1%)
    all_to_all x1, waiting for transfers between devices, shards(): lax.all_to_all(update_core(screened[None, None], 'occ'), 'vir', split_axi...  135 us
    all_to_all x1, blocking collectives, update_core(): lax.all_to_all(jnp.stack(jnp.split(t0, lax.axis_size(a_name), axis=3), ax...  104 us
    reduce_scatter x1, waiting for transfers between devices, shards(): lax.psum_scatter(lax.dot_general(int_slab, flat_rows, (((0,), (1,)), ((),...  87.3 us
    all_to_all x2, local copies, waits for them, and re-layouts, shards(): lax.all_to_all(update_core(screened[None, None], 'occ'), 'vir', split_axi...  23.1 us
    reshape x1, local copies, waits for them, and re-layouts, shards(): flat_rows = relaid.reshape(-1, occ_part * vir_part)  19.9 us
    reshape x1, local copies, waits for them, and re-layouts, update_core(): jnp.concatenate(lax.all_to_all(jnp.stack(jnp.split(t0, lax.axis_size(a_na...  12.5 us
    reshape x1, local copies, waits for them, and re-layouts, shards(): int_slab = integrals.reshape(occ_part * vir_part, col_total)  11.9 us
    reduce_scatter x1, waiting for transfers between devices, shards(): lax.psum_scatter(per_vir, 'occ', scatter_dimension=1, tiled=True)  11 us
  transfers between devices with their start and end apart: 3, of which 3 were waited for; matrix products, arithmetic and copies ran while one was open for 4% of the time, Pallas kernels for 0%

profile of v1, /device:TPU:0, one launch (start us, length us, event | category | flops | bytes accessed | tf_op | source)
XLA Modules:
  0.0 464.0 jit_solution(1362847301013523493)
XLA Ops:
  6.5 0.7 convert_element_type.3
  7.2 0.3 broadcast_in_dim.4
  7.5 1.0 mul.10
  8.5 7.5 %multiply_bitcast_fusion = bf16[1,1,8,240,2112]{4,3,2,1,0:T(8,128)(2,1)} fusion(bf16[8,240,2112]{2,1,0:T(8,128)(2,1)} %param.5, bf16[240,2112]{1,0:T(8,128)(2,1)S(1)} %mul.10), kind=kLoop, calls=%fused_computation.1 | loop fusion | flops 4055040 | bytes 17233920 | tf_op jit(solution)/shard_map/broadcast_in_dim | solution.py:26
  16.0 5.1 %slice_bitcast_fusion.1 = (bf16[1,1,1,8,120,2112]{5,4,3,2,1,0:T(8,128)(2,1)S(1)}, bf16[1,1,1,8,120,2112]{5,4,3,2,1,0:T(8,128)(2,1)}) fusion(bf16[1,1,8,240,2112]{4,3,2,1,0:T(8,128)(2,1)} %multiply_bitcast_fusion), kind=kLoop, calls=%fused_computation.3 | loop fusion | bytes 16220160 | tf_op jit(solution)/shard_map/stack | solution.py:10
  21.0 6.3 %pad_maximum_fusion = bf16[2,1,1,8,120,2112]{5,4,3,2,1,0:T(8,128)(2,1)} fusion(bf16[1,1,1,8,120,2112]{5,4,3,2,1,0:T(8,128)(2,1)} %get-tuple-element.6, bf16[1,1,1,8,120,2112]{5,4,3,2,1,0:T(8,128)(2,1)S(1)} %get-tuple-element.5), kind=kLoop, calls=%fused_computation | loop fusion | flops 4055040 | bytes 16220160 | tf_op jit(solution)/shard_map/stack | solution.py:10
  27.3 104.3 %all_to_all.20 = bf16[2,1,1,8,120,2112]{5,4,3,2,1,0:T(8,128)(2,1)} all-to-all(bf16[2,1,1,8,120,2112]{5,4,3,2,1,0:T(8,128)(2,1)} %pad_maximum_fusion), channel_id=1, replica_groups=mesh['occ'=2,'vir'=16] {'occ'}, dimensions={0} | all-to-all | bytes 16220160 | tf_op jit(solution)/shard_map/all_to_all | solution.py:9
  131.6 12.5 %copy.18 = bf16[2,1,8,120,2112]{3,2,0,1,4:T(8,128)(2,1)} copy(bf16[2,1,8,120,2112]{4,3,2,0,1:T(8,128)(2,1)} %bitcast.22) | data formatting | bytes 16220160 | tf_op jit(solution)/shard_map/reshape | solution.py:8
  144.1 6.2 %all-to-all-start.1 = ((bf16[2,1,8,120,2112]{3,2,0,1,4:T(8,128)(2,1)}), bf16[2,1,8,120,2112]{3,2,0,1,4:T(8,128)(2,1)}, u32[]{:S(2)}, u32[]{:S(2)}) async-start(bf16[2,1,8,120,2112]{3,2,0,1,4:T(8,128)(2,1)} %copy.18), calls=%async_computation.1 | async-start | bytes 17301504 | tf_op jit(solution)/shard_map/all_to_all | solution.py:25
  150.4 0.0 reduce-scatter.7.cloned.1.call-start
  150.4 8.2 %copy.21 = bf16[120,132,256]{2,1,0:T(8,128)(2,1)} copy(bf16[120,132,256]{2,0,1:T(8,128)(2,1)} %param.6) | data formatting | bytes 16220160 | tf_op args[1]
  158.6 11.9 %reshape.16 = bf16[15840,256]{1,0:T(8,128)(2,1)} reshape(bf16[120,132,256]{2,1,0:T(8,128)(2,1)} %copy.21) | data formatting | bytes 16220160 | tf_op jit(solution)/shard_map/reshape | solution.py:29
  170.6 135.1 %all-to-all-done.1 = bf16[2,1,8,120,2112]{3,2,0,1,4:T(8,128)(2,1)} async-done(((bf16[2,1,8,120,2112]{3,2,0,1,4:T(8,128)(2,1)}), bf16[2,1,8,120,2112]{3,2,0,1,4:T(8,128)(2,1)}, u32[]{:S(2)}, u32[]{:S(2)}) %all-to-all-start.1) | async-done | bytes 8110112 | tf_op jit(solution)/shard_map/all_to_all | solution.py:25
  305.7 7.2 %copy.19 = bf16[2,1,8,120,2112]{3,2,4,0,1:T(8,128)(2,1)} copy(bf16[2,1,8,120,2112]{3,2,0,1,4:T(8,128)(2,1)} %all-to-all-done.1) | data formatting | bytes 16220160 | tf_op jit(solution)/shard_map/all_to_all | solution.py:25
  312.8 15.9 %copy.20 = bf16[2,16,1,8,120,132]{5,4,3,1,0,2:T(8,128)(2,1)} copy(bf16[2,16,1,8,120,132]{4,3,5,1,0,2:T(8,128)(2,1)} %bitcast.21) | data formatting | bytes 16220160 | tf_op jit(solution)/shard_map/all_to_all | solution.py:25
  328.7 19.9 %reshape.15 = bf16[256,15840]{1,0:T(8,128)(2,1)} reshape(bf16[2,16,1,8,120,132]{5,4,3,1,0,2:T(8,128)(2,1)} %copy.20) | data formatting | bytes 16220160 | tf_op jit(solution)/shard_map/reshape | solution.py:28
  348.7 0.0 copy-start
  348.7 0.0 copy-start.1
  348.7 7.9 %convolution_bitcast_fusion = f32[256,256]{0,1:T(8,128)S(1)} fusion(bf16[256,15840]{1,0:T(8,128)(2,1)} %reshape.15, bf16[15840,256]{1,0:T(8,128)(2,1)} %reshape.16), kind=kOutput, calls=%fused_computation.4 | convolution fusion | flops 2076180480 | bytes 16482304 | tf_op jit(solution)/shard_map/dot_general | solution.py:31
  356.6 0.8 copy.23
  357.4 0.0 reduce-scatter.7.cloned.1.call-update
  357.4 0.0 reduce-scatter.5.cloned.1.call-start
  357.5 87.3 %reduce-scatter.7.cloned.1.call-done = f32[16,256]{1,0:T(8,128)} async-done(((f32[256,256]{1,0:T(8,128)}), f32[16,256]{1,0:T(8,128)}) %reduce-scatter.7.cloned.1.call-update) | async-done | bytes 16400 | tf_op jit(solution)/shard_map/reduce_scatter | solution.py:30
  444.8 0.0 reduce-scatter.5.cloned.1.call-update
  444.8 11.0 %reduce-scatter.5.cloned.1.call-done = f32[16,128]{1,0:T(8,128)} async-done(((f32[16,256]{1,0:T(8,128)}), f32[16,128]{1,0:T(8,128)}) %reduce-scatter.5.cloned.1.call-update) | async-done | bytes 8208 | tf_op jit(solution)/shard_map/reduce_scatter | solution.py:38
  455.8 0.0 copy-done
  455.8 0.0 copy-done.1
  455.8 1.4 bitcast_divide_fusion
Async XLA Ops:
  144.1 161.5 %all-to-all-start.1 = ((bf16[2,1,8,120,2112]{3,2,0,1,4:T(8,128)(2,1)}), bf16[2,1,8,120,2112]{3,2,0,1,4:T(8,128)(2,1)}, u32[]{:S(2)}, u32[]{:S(2)}) async-start(bf16[2,1,8,120,2112]{3,2,0,1,4:T(8,128)(2,1)} %copy.18), calls=%async_computation.1 | async-start | bytes 17301504 | tf_op jit(solution)/shard_map/all_to_all | solution.py:25
  150.4 294.4 %reduce-scatter.7.cloned.1.call-start = ((), (), s32[]{:S(2)}) async-start(), calls=%async_computation.5 | async-start | bytes 278528 | tf_op jit(solution)/shard_map/reduce_scatter | solution.py:30
  348.7 107.2 %copy-start = (f32[16]{0:T(128)S(1)}, f32[16]{0:T(128)}, u32[]{:S(2)}) copy-start(f32[16]{0:T(128)} %param.9) | copy-start | bytes 196
  348.7 107.2 %copy-start.1 = (f32[128]{0:T(128)S(1)}, f32[128]{0:T(128)}, u32[]{:S(2)}) copy-start(f32[128]{0:T(128)} %param.8) | copy-start | bytes 1540
  357.4 98.4 %reduce-scatter.5.cloned.1.call-start = ((), (), s32[]{:S(2)}) async-start(), calls=%async_computation.4 | async-start | bytes 24576 | tf_op jit(solution)/shard_map/reduce_scatter | solution.py:38
Sparse Core Ops, SparseCore 0:
  357.6 87.2 reduce-scatter.6
  447.0 8.7 reduce-scatter.4
